TPU v7x, 32 devices: a whole 2x2x4 slice. The times are simulated.
32 devices in a mesh: pool: 2 (over x), row: 8 (over z, y), col: 2 (over core).
Axes of the slice: x: 2, y: 2, z: 4, core: 2. Of those that a mesh axis runs over, the one named last changes fastest.
Arguments:
- grad_slots: bfloat16 [48, 256, 14336], P(('pool', 'row'), 'col'), parts along dimension 0, may hold values from -6 to 6
- block_owner: int32 [32], P('pool'), parts along dimension 0, may hold values from 0 to 7, as said below
- factor: bfloat16 [8192, 4096], P(('pool', 'col'), 'row'), parts along dimension 0, may hold values from -0.125 to 0.125
- pattern: int32 [16, 8], P('pool'), parts along dimension 0, may hold values from 0 to 1, as said below
Outputs:
- precond: bfloat16 [8192, 14336], P(('pool', 'col'), 'row'), parts along dimension 0
There are 2 independent parts, one for each index of `pool`. A program takes and returns all parts, laid end to end along the dimension named above; each array names one. Nothing has to cross between parts.
Inputs may be any that keep to these rules, and one draw needn't show every extreme that they name: `block_owner`: no trainer shard holds more than 3 blocks and one holds exactly 3; a shard keeps its blocks in its first slots in increasing block order, and the other slots are unused. `pattern`: 1 on the diagonal and 0 below it.
All inputs are finite; a program needn't handle non-finite values.
Results may differ from a plain program's by a relative error of at most 0.004.
Values may be sent and summed in bfloat16 or wider, within the bound.
A program may use at most 192 MiB of HBM per device.

v0:
```python
import jax
import jax.numpy as jnp
from jax import lax
from jax.sharding import PartitionSpec as P


def body(grad_slots, block_owner, factor, pattern):
    row_idx = lax.axis_index("row")
    col_idx = lax.axis_index("col")
    slot_cap = grad_slots.shape[0]
    block_total = block_owner.shape[0]
    received = lax.all_to_all(grad_slots, "row", split_axis=2, concat_axis=0, tiled=True)
    same_owner = block_owner[:, None] == block_owner[None, :]
    earlier = jnp.arange(block_total)[None, :] < jnp.arange(block_total)[:, None]
    owner_rank = jnp.sum(same_owner & earlier, axis=1)
    slot_of = block_owner * slot_cap + owner_rank
    picked = jnp.take(received, slot_of, axis=0)
    blocks = lax.all_gather(picked, "col", axis=1, tiled=True)
    grad_cols = blocks.reshape(-1, blocks.shape[2])
    half_rows, piece_width = factor.shape
    block_count = pattern.shape[0]
    total_rows = 2 * half_rows
    block_size = total_rows // block_count
    half_blocks = block_count // 2
    col_block = (row_idx * piece_width + jnp.arange(piece_width)) // block_size
    row_blocks = col_idx * half_blocks + jnp.arange(half_blocks)
    sel_cols = (jnp.arange(block_count)[:, None] == col_block[None, :]).astype(jnp.float32)
    pattern_cols = jnp.dot(pattern.astype(jnp.float32), sel_cols)
    sel_rows = (row_blocks[:, None] == jnp.arange(block_count)[None, :]).astype(jnp.float32)
    block_mask = jnp.dot(sel_rows, pattern_cols)
    keep_mask = block_mask > 0.5
    shaped = factor.reshape(half_blocks, block_size, piece_width)
    masked = jnp.where(keep_mask[:, None, :], shaped, jnp.zeros_like(shaped)).reshape(
        half_rows, piece_width
    )
    result = jnp.dot(
        lax.all_gather(masked, "row", axis=1, tiled=True),
        grad_cols,
        preferred_element_type=jnp.float32,
    )
    return result.astype(jnp.bfloat16)


def solution(mesh):
    placed = (
        P(("pool", "row"), "col", None),
        P("pool"),
        P(("pool", "col"), "row"),
        P("pool", None),
    )
    return jax.shard_map(
        body, mesh=mesh, in_specs=placed, out_specs=P(("pool", "col"), "row"), check_vma=False
    )
```

profile of v0, /device:TPU:0, one launch (start us, length us, event | category | flops | bytes accessed | tf_op | source)
XLA Modules:
  0.0 657.5 jit_solution(4763586861439865328)
XLA Ops:
  6.5 0.0 all-gather.3.cloned.1.call-start
  6.6 0.9 fusion.3
  7.5 3.1 bitcast_select_fusion
  10.6 0.0 all-gather.3.cloned.1.call-update
  10.6 22.4 %copy.10 = bf16[3,128,14336]{1,0,2:T(4,128)(2,1)} copy(bf16[3,128,14336]{2,1,0:T(8,128)(2,1)} %param.4) | data formatting | bytes 22020096 | tf_op args[0]
  33.0 0.0 copy-start
  33.0 7.4 %all-to-all-start = ((bf16[3,128,14336]{1,0,2:T(4,128)(2,1)}), bf16[3,128,14336]{1,0,2:T(4,128)(2,1)}, u32[]{:S(2)}, u32[]{:S(2)}) async-start(bf16[3,128,14336]{1,0,2:T(4,128)(2,1)} %copy.10), calls=%async_computation | async-start | bytes 29360128 | tf_op jit(solution)/shard_map/all_to_all | solution.py:12
  40.4 0.0 all-gather.5.cloned.1.call-start
  40.5 0.0 copy-done
  40.5 0.2 convert_reduce_fusion
  40.7 504.1 %all-to-all-done = bf16[3,128,14336]{1,0,2:T(4,128)(2,1)} async-done(((bf16[3,128,14336]{1,0,2:T(4,128)(2,1)}), bf16[3,128,14336]{1,0,2:T(4,128)(2,1)}, u32[]{:S(2)}, u32[]{:S(2)}) %all-to-all-start) | async-done | bytes 11010080 | tf_op jit(solution)/shard_map/all_to_all | solution.py:12
  544.8 12.4 %copy.11 = bf16[3,128,14336]{1,2,0:T(8,128)(2,1)} copy(bf16[3,128,14336]{1,0,2:T(4,128)(2,1)} %all-to-all-done) | data formatting | bytes 22020096 | tf_op jit(solution)/shard_map/all_to_all | solution.py:12
  557.2 14.2 %copy.12 = bf16[8,3,128,1792]{3,2,1,0:T(8,128)(2,1)} copy(bf16[8,3,128,1792]{2,3,0,1:T(8,128)(2,1)} %bitcast.9) | data formatting | bytes 22020096 | tf_op jit(solution)/shard_map/all_to_all | solution.py:12
  571.3 8.2 %gather_fusion = bf16[16,128,1792]{2,1,0:T(8,128)(2,1)} fusion(bf16[24,128,1792]{2,1,0:T(8,128)(2,1)} %bitcast.10, s32[1024]{0:T(1024)S(1)} %pad_clamp_fusion), kind=kCustom, calls=%fused_computation | custom fusion | bytes 14680128 | tf_op jit(solution)/shard_map/jit(_take)/gather | solution.py:17
  579.5 6.9 %broadcast_select_fusion = bf16[16,128,1792]{2,1,0:T(8,128)(2,1)} fusion(bf16[16,128,1792]{2,1,0:T(8,128)(2,1)} %gather_fusion, pred[16]{0:T(512)(128)(4,1)S(1)} %get-tuple-element.5), kind=kLoop, calls=%fused_computation.2 | loop fusion | flops 3670016 | bytes 14680080 | tf_op jit(solution)/shard_map/jit(_take)/select_n | solution.py:17
  586.4 0.0 all-gather.5.cloned.1.call-update
  586.5 0.0 all-gather.3.cloned.1.call-done
  586.5 25.5 %all-gather.5.cloned.1.call-done = bf16[16,256,1792]{2,1,0:T(8,128)(2,1)} async-done(((bf16[16,128,1792]{2,1,0:T(8,128)(2,1)}), bf16[16,256,1792]{2,1,0:T(8,128)(2,1)}) %all-gather.5.cloned.1.call-update) | async-done | bytes 14680080 | tf_op jit(solution)/shard_map/all_gather | solution.py:18
  612.0 38.6 %convolution_convert_fusion = bf16[2048,1792]{1,0:T(8,128)(2,1)} fusion(bf16[2048,4096]{1,0:T(8,128)(2,1)} %all-gather.3.cloned.1.call-done, bf16[4096,1792]{1,0:T(8,128)(2,1)} %bitcast.11), kind=kOutput, calls=%fused_computation.1 | convolution fusion | flops 30068441088 | bytes 38797312 | tf_op jit(solution)/shard_map/dot_general | solution.py:36
  (4 shorter events, 0.0 us)
Async XLA Ops:
  6.5 579.9 %all-gather.3.cloned.1.call-start = ((), (), s32[]{:S(2)}) async-start(), calls=%async_computation.1 | async-start | bytes 18874368 | tf_op jit(solution)/shard_map/all_gather | solution.py:37
  33.0 7.5 %copy-start = (s32[16]{0:T(128)S(1)}, s32[16]{0:T(128)}, u32[]{:S(2)}) copy-start(s32[16]{0:T(128)} %param.5) | copy-start | bytes 196
  33.0 511.8 %all-to-all-start = ((bf16[3,128,14336]{1,0,2:T(4,128)(2,1)}), bf16[3,128,14336]{1,0,2:T(4,128)(2,1)}, u32[]{:S(2)}, u32[]{:S(2)}) async-start(bf16[3,128,14336]{1,0,2:T(4,128)(2,1)} %copy.10), calls=%async_computation | async-start | bytes 29360128 | tf_op jit(solution)/shard_map/all_to_all | solution.py:12
  40.4 571.6 %all-gather.5.cloned.1.call-start = ((), (), s32[]{:S(2)}) async-start(), calls=%async_computation.2 | async-start | bytes 22020096 | tf_op jit(solution)/shard_map/all_gather | solution.py:18
Sparse Core Ops, SparseCore 0:
  10.7 526.6 all-gather.2
  586.6 25.3 all-gather.4
where the time goes:
time: 659 us; the launch traced here: 657 us
  waiting for transfers between devices  530 us (80%)
  local copies, waits for them, and re-layouts  57.2 us (9%)
  matrix products  39.5 us (6%)
  between operations  13.4 us (2%)
  other arithmetic  10.2 us (2%)
  starting transfers between devices  7.44 us (1%)
    all_to_all x1, waiting for transfers between devices, body(): lax.all_to_all(grad_slots, 'row', split_axis=2, concat_axis=0, tiled=True)  504 us
    dot_general x1, matrix products, body(): jnp.dot(lax.all_gather(masked, 'row', axis=1, tiled=True), grad_cols, pre...  38.6 us
    all_to_all x2, local copies, waits for them, and re-layouts, body(): lax.all_to_all(grad_slots, 'row', split_axis=2, concat_axis=0, tiled=True)  26.6 us
    all_gather x1, waiting for transfers between devices, body(): blocks = lax.all_gather(picked, 'col', axis=1, tiled=True)  25.5 us
    unnamed x3, local copies, waits for them, and re-layouts  22.4 us
  transfers between devices with their start and end apart: 3, of which 2 were waited for; matrix products, arithmetic and copies ran while one was open for 10% of the time, Pallas kernels for 0%

commit v1 on v0

--- a/solution.py
+++ b/solution.py
@@ -5,11 +5,31 @@
 
 
 def body(grad_slots, block_owner, factor, pattern):
+
+    def bring_the_records(base_x, in_dim, join_dim):
+        far_arr, outcome_arr = (lax.axis_size("row"), lax.axis_index("row"))
+        local_out = list(base_x.shape)
+        then = base_x.shape[in_dim] // far_arr
+        local_out[in_dim] = then
+        latest = local_out[join_dim]
+        local_out[join_dim] = latest * far_arr
+        big = jnp.zeros(local_out, base_x.dtype)
+        for hop_no in range(far_arr):
+            e_next = lax.dynamic_slice_in_dim(
+                base_x, (outcome_arr ^ hop_no) * then, then, axis=in_dim
+            )
+            if hop_no:
+                e_next = lax.ppermute(e_next, "row", [(t, t ^ hop_no) for t in range(far_arr)])
+            big = lax.dynamic_update_slice_in_dim(
+                big, e_next, (outcome_arr ^ hop_no) * latest, axis=join_dim
+            )
+        return big
+
     row_idx = lax.axis_index("row")
     col_idx = lax.axis_index("col")
     slot_cap = grad_slots.shape[0]
     block_total = block_owner.shape[0]
-    received = lax.all_to_all(grad_slots, "row", split_axis=2, concat_axis=0, tiled=True)
+    received = bring_the_records(grad_slots, 2, 0)
     same_owner = block_owner[:, None] == block_owner[None, :]
     earlier = jnp.arange(block_total)[None, :] < jnp.arange(block_total)[:, None]
     owner_rank = jnp.sum(same_owner & earlier, axis=1)

time: 659 us -> 585 us (0.89)
  waiting for transfers between devices: 530 us -> 474 us
  local copies, waits for them, and re-layouts: 57.2 us -> 35.4 us
    all_to_all x1 -> x0, waiting for transfers between devices: 504 us -> none  [body(): lax.all_to_all(grad_slots, 'row', split_axis=2, concat_axis=0, tiled=True)]
    all_gather x1, waiting for transfers between devices: 0.02 us -> 231 us  [body(): lax.all_gather(masked, 'row', axis=1, tiled=True)]
    ppermute x0 -> x7, waiting for transfers between devices: none -> 165 us  [bring_the_records(): lax.ppermute(e_next, 'row', [(t, t ^ hop_no) for t in range(far_arr)])]
    all_gather x1, waiting for transfers between devices: 25.5 us -> 78.1 us  [body(): blocks = lax.all_gather(picked, 'col', axis=1, tiled=True)]
    all_to_all x2 -> x0, local copies, waits for them, and re-layouts: 26.6 us -> none  [body(): lax.all_to_all(grad_slots, 'row', split_axis=2, concat_axis=0, tiled=True)]
    unnamed x3 -> x6, local copies, waits for them, and re-layouts: 22.4 us -> 1.08 us
    ppermute x0 -> x7, starting transfers between devices: none -> 13.6 us  [bring_the_records(): lax.ppermute(e_next, 'row', [(t, t ^ hop_no) for t in range(far_arr)])]
    dynamic_update_slice x0 -> x7, local copies, waits for them, and re-layouts: none -> 12.4 us  [bring_the_records(): lax.dynamic_update_slice_in_dim(big, e_next, (outcome_arr ^ hop_no) * lat...]
  transfers between devices with their start and end apart: 3 -> 9, of which waited for: 2 -> 6; matrix products, arithmetic and copies ran while one was open for 10% -> 2% of each run, Pallas kernels for 0% -> 0%
where the time goes in v1:
time: 585 us; the launch traced here: 584 us
  waiting for transfers between devices  474 us (81%)
  matrix products  39 us (7%)
  local copies, waits for them, and re-layouts  35.4 us (6%)
  starting transfers between devices  13.7 us (2%)
  between operations  13.4 us (2%)
  other arithmetic  8.56 us (1%)
    all_gather x1, waiting for transfers between devices, body(): lax.all_gather(masked, 'row', axis=1, tiled=True)  231 us
    ppermute x7, waiting for transfers between devices, bring_the_records(): lax.ppermute(e_next, 'row', [(t, t ^ hop_no) for t in range(far_arr)])  165 us
    all_gather x1, waiting for transfers between devices, body(): blocks = lax.all_gather(picked, 'col', axis=1, tiled=True)  78.1 us
    dot_general x1, matrix products, body(): jnp.dot(lax.all_gather(masked, 'row', axis=1, tiled=True), grad_cols, pre...  38.6 us
    ppermute x7, starting transfers between devices, bring_the_records(): lax.ppermute(e_next, 'row', [(t, t ^ hop_no) for t in range(far_arr)])  13.6 us
    dynamic_update_slice x7, local copies, waits for them, and re-layouts, bring_the_records(): lax.dynamic_update_slice_in_dim(big, e_next, (outcome_arr ^ hop_no) * lat...  12.4 us
  transfers between devices with their start and end apart: 9, of which 6 were waited for; matrix products, arithmetic and copies ran while one was open for 2% of the time, Pallas kernels for 0%

profile of v1, /device:TPU:0, one launch (start us, length us, event | category | flops | bytes accessed | tf_op | source)
XLA Modules:
  0.0 584.3 jit_solution(2557090740590469201)
XLA Ops:
  6.5 5.4 broadcast_in_dim.41
  11.9 8.4 %constant_dynamic-slice_fusion = (bf16[3,128,1792]{2,1,0:T(8,128)(2,1)}, bf16[3,128,1792]{2,1,0:T(8,128)(2,1)}, bf16[3,128,1792]{2,1,0:T(8,128)(2,1)}, bf16[3,12...) fusion(bf16[3,128,14336]{2,1,0:T(8,128)(2,1)} %param.4, ...), kind=kLoop, calls=%fused_computation.16 | loop fusion | bytes 22020132 | tf_op jit(solution)/shard_map/dynamic_slice | solution.py:18
  20.3 3.0 collective-permute-start
  23.3 1.6 collective-permute-start.1
  24.9 3.0 collective-permute-start.3
  27.9 1.3 collective-permute-start.4
  29.3 24.4 %collective-permute-done = bf16[3,128,1792]{2,1,0:T(8,128)(2,1)} collective-permute-done((bf16[3,128,1792]{2,1,0:T(8,128)(2,1)}, bf16[3,128,1792]{2,1,0:T(8,128)(2,1)}, u32[]{:S(2)}, u32[]{:S(2)}) %collective-permute-start) | collective-permute-done | bytes 1376288 | tf_op jit(solution)/shard_map/ppermute | solution.py:22
  53.8 3.8 collective-permute-start.5
  57.6 57.1 %collective-permute-done.1 = bf16[3,128,1792]{2,1,0:T(8,128)(2,1)} collective-permute-done((bf16[3,128,1792]{2,1,0:T(8,128)(2,1)}, bf16[3,128,1792]{2,1,0:T(8,128)(2,1)}, u32[]{:S(2)}, u32[]{:S(2)}) %collective-permute-start.1) | collective-permute-done | bytes 1376288 | tf_op jit(solution)/shard_map/ppermute | solution.py:22
  115.8 2.5 constant_dynamic-update-slice_fusion.5
  118.3 2.5 constant_dynamic-update-slice_fusion.4
  120.8 21.1 %collective-permute-done.2 = bf16[3,128,1792]{2,1,0:T(8,128)(2,1)} collective-permute-done((bf16[3,128,1792]{2,1,0:T(8,128)(2,1)}, bf16[3,128,1792]{2,1,0:T(8,128)(2,1)}, u32[]{:S(2)}, u32[]{:S(2)}) %collective-permute-start.2) | collective-permute-done | bytes 1376288 | tf_op jit(solution)/shard_map/ppermute | solution.py:22
  141.9 2.5 constant_dynamic-update-slice_fusion.3
  144.4 1.2 constant_dynamic-update-slice_fusion.2
  145.6 62.3 %collective-permute-done.4 = bf16[3,128,1792]{2,1,0:T(8,128)(2,1)S(1)} collective-permute-done((bf16[3,128,1792]{2,1,0:T(8,128)(2,1)}, bf16[3,128,1792]{2,1,0:T(8,128)(2,1)S(1)}, u32[]{:S(2)}, u32[]{:S(2)}) %collective-permute-start.4) | collective-permute-done | bytes 1376288 | tf_op jit(solution)/shard_map/ppermute | solution.py:22
  207.9 1.2 constant_dynamic-update-slice_fusion.1
  209.1 1.3 constant_dynamic-update-slice_fusion
  210.4 1.2 constant_dynamic-update-slice_fusion.6
  211.5 8.2 %gather_fusion = bf16[16,128,1792]{2,1,0:T(8,128)(2,1)} fusion(bf16[24,128,1792]{2,1,0:T(8,128)(2,1)} %constant_dynamic-update-slice_fusion.6, s32[1024]{0:T(1024)S(1)} %pad_clamp_fusion), kind=kCustom, calls=%fused_computation | custom fusion | bytes 14680128 | tf_op jit(solution)/shard_map/jit(_take)/gather | solution.py:37
  219.7 6.9 %broadcast_select_fusion = bf16[16,128,1792]{2,1,0:T(8,128)(2,1)} fusion(bf16[16,128,1792]{2,1,0:T(8,128)(2,1)} %gather_fusion, pred[16]{0:T(512)(128)(4,1)S(1)} %get-tuple-element.5), kind=kLoop, calls=%fused_computation.2 | loop fusion | flops 3670016 | bytes 14680080 | tf_op jit(solution)/shard_map/jit(_take)/select_n | solution.py:37
  228.2 1.4 bitcast_select_fusion
  229.7 78.1 %all-gather.5.cloned.1.call-done = bf16[16,256,1792]{2,1,0:T(8,128)(2,1)} async-done(((bf16[16,128,1792]{2,1,0:T(8,128)(2,1)}), bf16[16,256,1792]{2,1,0:T(8,128)(2,1)}) %all-gather.5.cloned.1.call-update) | async-done | bytes 14680080 | tf_op jit(solution)/shard_map/all_gather | solution.py:38
  307.8 231.0 %all-gather.3.cloned.1.call-done = bf16[2048,4096]{1,0:T(8,128)(2,1)} async-done(((bf16[2048,512]{1,0:T(8,128)(2,1)}), bf16[2048,4096]{1,0:T(8,128)(2,1)}) %all-gather.3.cloned.1.call-update) | async-done | bytes 16777232 | tf_op jit(solution)/shard_map/all_gather | solution.py:57
  538.8 38.6 %convolution_convert_fusion = bf16[2048,1792]{1,0:T(8,128)(2,1)} fusion(bf16[2048,4096]{1,0:T(8,128)(2,1)} %all-gather.3.cloned.1.call-done, bf16[4096,1792]{1,0:T(8,128)(2,1)} %bitcast.5), kind=kOutput, calls=%fused_computation.1 | convolution fusion | flops 30068441088 | bytes 38797312 | tf_op jit(solution)/shard_map/dot_general | solution.py:56
  (21 shorter events, 2.8 us)
Async XLA Ops:
  6.5 301.3 %all-gather.5.cloned.1.call-start = ((), (), s32[]{:S(2)}) async-start(), calls=%async_computation.1 | async-start | bytes 22020096 | tf_op jit(solution)/shard_map/all_gather | solution.py:38
  11.9 17.3 %copy-start.1 = (s32[16]{0:T(128)S(1)}, s32[16]{0:T(128)}, u32[]{:S(2)}) copy-start(s32[16]{0:T(128)} %param.5) | copy-start | bytes 196
  20.3 33.5 %collective-permute-start = (bf16[3,128,1792]{2,1,0:T(8,128)(2,1)}, bf16[3,128,1792]{2,1,0:T(8,128)(2,1)}, u32[]{:S(2)}, u32[]{:S(2)}) collective-permute-start(bf16[3,128,1792]{2,1,0:T(8,128)(2,1)} %get-tuple-element.12), channel_id=1, source_target_pairs={{0,2},{2,0},{4,6},{6,4},{8,10},{10,8},{12,14},{14,12},{1,3},{3,1},... | collective-permute-start | bytes 4128776 | tf_op jit(solution)/shard_map/ppermute | solution.py:22
  23.3 91.5 %collective-permute-start.1 = (bf16[3,128,1792]{2,1,0:T(8,128)(2,1)}, bf16[3,128,1792]{2,1,0:T(8,128)(2,1)}, u32[]{:S(2)}, u32[]{:S(2)}) collective-permute-start(bf16[3,128,1792]{2,1,0:T(8,128)(2,1)} %get-tuple-element.11), channel_id=1, source_target_pairs={{0,4},{2,6},{4,0},{6,2},{8,12},{10,14},{12,8},{14,10},{1,5},{3,7},... | collective-permute-start | bytes 4128776 | tf_op jit(solution)/shard_map/ppermute | solution.py:22
  24.9 117.0 %collective-permute-start.2 = (bf16[3,128,1792]{2,1,0:T(8,128)(2,1)}, bf16[3,128,1792]{2,1,0:T(8,128)(2,1)}, u32[]{:S(2)}, u32[]{:S(2)}) collective-permute-start(bf16[3,128,1792]{2,1,0:T(8,128)(2,1)} %get-tuple-element.10), channel_id=1, source_target_pairs={{0,6},{2,4},{4,2},{6,0},{8,14},{10,12},{12,10},{14,8},{1,7},{3,5},... | collective-permute-start | bytes 4128776 | tf_op jit(solution)/shard_map/ppermute | solution.py:22
  24.9 119.6 %collective-permute-start.3 = (bf16[3,128,1792]{2,1,0:T(8,128)(2,1)}, bf16[3,128,1792]{2,1,0:T(8,128)(2,1)S(1)}, u32[]{:S(2)}, u32[]{:S(2)}) collective-permute-start(bf16[3,128,1792]{2,1,0:T(8,128)(2,1)} %get-tuple-element.9), channel_id=1, source_target_pairs={{0,8},{2,10},{4,12},{6,14},{8,0},{10,2},{12,4},{14,6},{1,9},{3,11}... | collective-permute-start | bytes 4128776 | tf_op jit(solution)/shard_map/ppermute | solution.py:22
  27.9 180.1 %collective-permute-start.4 = (bf16[3,128,1792]{2,1,0:T(8,128)(2,1)}, bf16[3,128,1792]{2,1,0:T(8,128)(2,1)S(1)}, u32[]{:S(2)}, u32[]{:S(2)}) collective-permute-start(bf16[3,128,1792]{2,1,0:T(8,128)(2,1)} %get-tuple-element.8), channel_id=1, source_target_pairs={{0,10},{2,8},{4,14},{6,12},{8,2},{10,0},{12,6},{14,4},{1,11},{3,9}... | collective-permute-start | bytes 4128776 | tf_op jit(solution)/shard_map/ppermute | solution.py:22
  53.8 155.3 %collective-permute-start.5 = (bf16[3,128,1792]{2,1,0:T(8,128)(2,1)}, bf16[3,128,1792]{2,1,0:T(8,128)(2,1)S(1)}, u32[]{:S(2)}, u32[]{:S(2)}) collective-permute-start(bf16[3,128,1792]{2,1,0:T(8,128)(2,1)} %get-tuple-element.14), channel_id=1, source_target_pairs={{0,12},{2,14},{4,8},{6,10},{8,4},{10,6},{12,0},{14,2},{1,13},{3,15... | collective-permute-start | bytes 4128776 | tf_op jit(solution)/shard_map/ppermute | solution.py:22
  114.8 95.6 %collective-permute-start.6 = (bf16[3,128,1792]{2,1,0:T(8,128)(2,1)}, bf16[3,128,1792]{2,1,0:T(8,128)(2,1)S(1)}, u32[]{:S(2)}, u32[]{:S(2)}) collective-permute-start(bf16[3,128,1792]{2,1,0:T(8,128)(2,1)} %get-tuple-element.7), channel_id=1, source_target_pairs={{0,14},{2,12},{4,10},{6,8},{8,6},{10,4},{12,2},{14,0},{1,15},{3,13... | collective-permute-start | bytes 4128776 | tf_op jit(solution)/shard_map/ppermute | solution.py:22
  226.6 0.7 copy-start.2
  226.6 1.6 copy-start
  226.7 312.1 %all-gather.3.cloned.1.call-start = ((), (), s32[]{:S(2)}) async-start(), calls=%async_computation | async-start | bytes 18874368 | tf_op jit(solution)/shard_map/all_gather | solution.py:57
Sparse Core Ops, SparseCore 0:
  226.8 80.9 all-gather.4
  309.9 228.9 all-gather.2
